TPU v7x, 32 devices: a whole 2x2x4 slice. The times are simulated.
32 devices in a mesh: group: 4 (over y, x), inner: 8 (over z, core).
Axes of the slice: x: 2, y: 2, z: 4, core: 2. Of those that a mesh axis runs over, the one named last changes fastest.
Arguments:
- node_feats: bfloat16 [196608, 256], P(('group', 'inner')), may hold values from -6 to 6
- adj_tiles: bfloat16 [196608, 512], P(('group', 'inner')), may hold values from -0.25 to 0.25
- live_clusters: int32 [32], P(('group', 'inner')), may hold values from 4 to 12, as said below
- req_rows: int32 [32, 32, 16], P(('group', 'inner')), may hold values from 0 to 6143
- req_count: int32 [32, 32], P(('group', 'inner')), may hold values from 0 to 16, as said below
- req_target: int32 [32, 32, 16], P(('group', 'inner')), may hold values from 0 to 6143
- req_weight: float32 [32, 32, 16], P(('group', 'inner')), may hold values from 0.05 to 1
- hist_emb: bfloat16 [196608, 256], P(('group', 'inner')), may hold values from -6 to 6
- hist_grad: bfloat16 [196608, 256], P(('group', 'inner')), may hold values from -6 to 6
- layer_weight: bfloat16 [256, 256], replicated, may hold values from -0.375 to 0.375
- layer_bias: float32 [256], replicated, may hold values from -4 to 4
- cotangent: bfloat16 [196608, 256], P(('group', 'inner')), may hold values from -6 to 6
Outputs:
- input_grad: bfloat16 [196608, 256], P(('group', 'inner'))
- weight_grad: float32 [256, 256], replicated
- bias_grad: float32 [256], replicated
- owner_grad: bfloat16 [196608, 256], P(('group', 'inner'))
Inputs may be any that keep to these rules, and one draw needn't show every extreme that they name: `live_clusters`: some device has all 12 cluster slots filled and some has only the fewest. `req_count`: in every draw each requesting device fills all 16 slots to some owner, and some owner receives 16 used slots from every device.
All inputs are finite; a program needn't handle non-finite values.
Results may differ from a plain program's by a relative error of at most 0.0063.
Values may be sent and summed in bfloat16 or wider, within the bound.
A program may use at most 128 MiB of HBM per device.

v0:
```python
import math
import jax
import jax.numpy as jnp
from jax import lax
from jax.sharding import PartitionSpec as P


def gelu_slope(values):
    root_coef = math.sqrt(2.0 / math.pi)
    cube_coef = 0.044715
    tangent = jnp.tanh(root_coef * (values + cube_coef * values * values * values))
    return 0.5 * (1.0 + tangent) + 0.5 * values * (1.0 - tangent * tangent) * root_coef * (
        1.0 + 3.0 * cube_coef * values * values
    )


def on_device(
    node_feats,
    adj_tiles,
    live_clusters,
    req_rows,
    req_count,
    req_target,
    req_weight,
    hist_emb,
    hist_grad,
    layer_weight,
    layer_bias,
    cotangent,
):
    nodes_dev, width = node_feats.shape
    cluster = adj_tiles.shape[1]
    clusters = nodes_dev // cluster
    asked = req_rows[0]
    peers, slots = asked.shape
    groups = lax.axis_size("group")
    members = lax.axis_size("inner")
    slot_used = jnp.arange(slots)[None, :] < req_count[0][:, None]
    slot_scale = jnp.where(slot_used, req_weight[0], jnp.float32(0.0))
    target_ids = req_target[0]
    targets = target_ids.reshape(-1)
    wanted = lax.all_to_all(asked, ("group", "inner"), split_axis=0, concat_axis=0, tiled=True)
    emb_rows = hist_emb[wanted]
    grad_rows = hist_grad[wanted]
    got_emb = lax.all_to_all(emb_rows, ("group", "inner"), split_axis=0, concat_axis=0, tiled=True)
    got_grad = lax.all_to_all(
        grad_rows, ("group", "inner"), split_axis=0, concat_axis=0, tiled=True
    )
    weights_col = slot_scale.reshape(-1, 1)
    adj_blocks = adj_tiles.reshape(clusters, cluster, cluster)
    local_sum = jnp.einsum(
        "cij,cjf->cif",
        adj_blocks,
        node_feats.reshape(clusters, cluster, width),
        preferred_element_type=jnp.float32,
    ).reshape(nodes_dev, width)
    comp_emb = jax.ops.segment_sum(
        weights_col * got_emb.reshape(-1, width).astype(jnp.float32),
        targets,
        num_segments=nodes_dev,
    )
    aggregate = (local_sum + comp_emb).astype(jnp.bfloat16)
    pre_act = jnp.dot(aggregate, layer_weight, preferred_element_type=jnp.float32) + layer_bias
    live_rows = (jnp.arange(nodes_dev) // cluster < live_clusters[0]).astype(jnp.float32)[:, None]
    grad_pre = cotangent.astype(jnp.float32) * gelu_slope(pre_act) * live_rows
    grad_low = grad_pre.astype(jnp.bfloat16)
    weight_part = jnp.einsum("nf,ng->fg", aggregate, grad_low, preferred_element_type=jnp.float32)
    bias_part = jnp.sum(grad_pre, axis=0)
    feat_grad = jnp.dot(grad_low, layer_weight.T, preferred_element_type=jnp.float32).astype(
        jnp.bfloat16
    )
    message = (slot_scale[:, :, None] * feat_grad[target_ids].astype(jnp.float32)).astype(
        jnp.bfloat16
    )
    arrived = lax.all_to_all(message, ("group", "inner"), split_axis=0, concat_axis=0, tiled=True)
    owner_grad = jax.ops.segment_sum(
        arrived.reshape(-1, width).astype(jnp.float32), wanted.reshape(-1), num_segments=nodes_dev
    ).astype(jnp.bfloat16)
    comp_grad = jax.ops.segment_sum(
        weights_col * got_grad.reshape(-1, width).astype(jnp.float32),
        targets,
        num_segments=nodes_dev,
    ).astype(jnp.bfloat16)
    back_sum = jnp.einsum(
        "cji,cjf->cif",
        adj_blocks,
        feat_grad.reshape(clusters, cluster, width),
        preferred_element_type=jnp.float32,
    ).reshape(nodes_dev, width)
    back_sum = back_sum + jnp.dot(comp_grad, layer_weight.T, preferred_element_type=jnp.float32)
    input_grad = (back_sum * live_rows).astype(jnp.bfloat16)
    weight_sum, bias_sum = lax.psum((weight_part, bias_part), ("group", "inner"))
    norm_factor = float(nodes_dev * groups * members) ** (-0.5)
    return (input_grad, weight_sum * norm_factor, bias_sum * norm_factor, owner_grad)


def solution(mesh):
    return jax.shard_map(
        on_device,
        mesh=mesh,
        in_specs=(
            P(("group", "inner"), None),
            P(("group", "inner"), None),
            P(("group", "inner")),
            P(("group", "inner"), None, None),
            P(("group", "inner"), None),
            P(("group", "inner"), None, None),
            P(("group", "inner"), None, None),
            P(("group", "inner"), None),
            P(("group", "inner"), None),
            P(),
            P(),
            P(("group", "inner"), None),
        ),
        out_specs=(P(("group", "inner"), None), P(), P(), P(("group", "inner"), None)),
        check_vma=False,
    )
```

profile of v0, /device:TPU:0, one launch (start us, length us, event | category | flops | bytes accessed | tf_op | source)
XLA Modules:
  0.0 225.8 jit_solution(15960307121424035594)
XLA Ops:
  7.2 0.0 copy-start
  7.2 1.5 copy.31
  8.7 7.3 %all-to-all-start = ((s32[32,1,16]{2,1,0:T(1,128)}), s32[32,1,16]{2,1,0:T(1,128)S(1)}, u32[]{:S(2)}, u32[]{:S(2)}) async-start(s32[32,1,16]{2,1,0:T(1,128)} %bitcast.4), calls=%async_computation | async-start | bytes 32768 | tf_op jit(solution)/shard_map/all_to_all | solution.py:42
  16.0 0.7 iota_compare_fusion
  16.7 0.7 bitcast_select_fusion
  17.4 0.8 copy.30
  18.8 0.1 copy.29
  18.9 0.1 lt.61
  19.0 0.8 copy.28
  19.8 0.1 reshape.183
  19.9 0.1 squeeze.12
  19.9 0.6 fusion.28
  20.5 0.0 copy-start.7
  20.6 0.1 reshape.191
  20.6 0.0 copy-start.8
  20.6 0.7 copy.34
  21.3 1.8 all-to-all-done
  23.1 0.0 copy-start.5
  23.1 0.1 reshape.167
  23.2 4.5 %gather_fusion = bf16[512,256]{1,0:T(8,128)(2,1)} fusion(bf16[6144,256]{1,0:T(8,128)(2,1)} %param.19, s32[1024]{0:T(1024)S(1)} %pad_clamp_fusion.1), kind=kCustom, calls=%fused_computation | custom fusion | bytes 526336 | tf_op jit(solution)/shard_map/gather | solution.py:43
  27.7 0.0 copy-done.5
  27.7 4.1 %all-to-all-start.1 = ((bf16[32,16,256]{2,1,0:T(8,128)(2,1)}), bf16[32,16,256]{2,1,0:T(8,128)(2,1)S(1)}, u32[]{:S(2)}, u32[]{:S(2)}) async-start(bf16[32,16,256]{2,1,0:T(8,128)(2,1)} %bitcast.48), calls=%async_computation.1 | async-start | bytes 524288 | tf_op jit(solution)/shard_map/all_to_all | solution.py:45
  31.8 0.0 copy-done
  31.8 7.2 %fusion.30 = f32[12,512,256]{2,1,0:T(8,128)} fusion(bf16[12,512,512]{2,1,0:T(8,128)(2,1)} %bitcast.40, bf16[12,512,256]{2,1,0:T(8,128)(2,1)S(1)} %bitcast.39), kind=kOutput, calls=%fused_computation.58 | convolution fusion | flops 1610612736 | bytes 15728640 | tf_op jit(solution)/shard_map/cij,cjf->cif/dot_general | solution.py:51
  39.0 0.0 copy-start.4
  39.0 0.5 broadcast.135
  39.5 2.0 reduce.3
  41.5 1.4 reshape.207
  42.9 4.5 %gather_fusion.1 = bf16[512,256]{1,0:T(8,128)(2,1)} fusion(bf16[6144,256]{1,0:T(8,128)(2,1)} %param.20, s32[1024]{0:T(1024)S(1)} %pad_clamp_fusion.1), kind=kCustom, calls=%fused_computation.1 | custom fusion | bytes 526336 | tf_op jit(solution)/shard_map/gather | solution.py:44
  47.4 0.0 all-to-all-done.1
  47.4 0.0 copy-start.3
  47.4 0.7 copy-done.3
  48.1 5.8 %all-to-all-start.2 = ((bf16[32,16,256]{2,1,0:T(8,128)(2,1)}), bf16[32,16,256]{2,1,0:T(8,128)(2,1)S(1)}, u32[]{:S(2)}, u32[]{:S(2)}) async-start(bf16[32,16,256]{2,1,0:T(8,128)(2,1)} %bitcast.46), calls=%async_computation.2 | async-start | bytes 524288 | tf_op jit(solution)/shard_map/all_to_all | solution.py:46
  54.0 0.0 all-reduce.2.cloned.1.call-start
  54.0 0.0 copy-done.7
  54.0 0.0 copy-done.8
  54.0 9.0 %scatter_custom_fusion = f32[6144,256]{1,0:T(8,128)} fusion(f32[6144,256]{1,0:T(8,128)} %bitcast.42, s32[512]{0:T(512)S(1)} %reshape.191, bf16[512,256]{1,0:T(8,128)(2,1)} %bitcast.47, f32[512]{0:T(512)S(1)} %broadcast_select_fusion), kind=kCustom, calls=%fused_computation.36 | custom fusion | flops 393216 | bytes 6555648 | tf_op jit(solution)/shard_map/scatter-add | solution.py:57
  63.0 0.0 copy-done.4
  63.0 0.0 copy-start.1
  63.0 8.5 %fusion.29 = (f32[256]{0:T(256)}, bf16[6144,256]{1,0:T(8,128)(2,1)S(1)}) fusion(f32[6144]{0:T(1024)} %fusion.28, f32[256]{0:T(256)} %param.22, bf16[256,256]{1,0:T(8,128)(2,1)S(1)} %copy-done.4, f32[6144,256]{1,0:T(8,128)} %scatter_custom_fusion, bf16[6144,256]{1,0:T(8,128)(2,1)} %param.23), kind=kOutput, calls=%fused_computation.57 | convolution fusion | flops 843054848 | bytes 12740608 | tf_op jit(solution)/shard_map/dot_general | solution.py:63
  71.4 0.0 copy-start.2
  71.4 1.7 copy-done.2
  73.1 0.0 copy-done.1
  73.1 1.7 fusion.14
  74.8 4.6 %convolution_convert_fusion = bf16[6144,256]{1,0:T(8,128)(2,1)} fusion(bf16[256,256]{1,0:T(8,128)(2,1)S(1)} %copy-done.4, bf16[6144,256]{1,0:T(8,128)(2,1)} %copy-done.2), kind=kOutput, calls=%fused_computation.12 | convolution fusion | flops 806879232 | bytes 6422528 | tf_op jit(solution)/shard_map/dot_general | solution.py:69
  79.4 0.0 all-reduce.2.cloned.1.call-update
  79.4 8.2 %convolution_bitcast_fusion = f32[12,512,256]{1,2,0:T(8,128)} fusion(bf16[12,512,256]{2,1,0:T(8,128)(2,1)} %bitcast.43, bf16[12,512,512]{2,1,0:T(8,128)(2,1)} %bitcast.41), kind=kOutput, calls=%fused_computation.25 | convolution fusion | flops 1610612736 | bytes 15728640 | tf_op jit(solution)/shard_map/cji,cjf->cif/dot_general | solution.py:84
  87.7 4.5 %gather_fusion.2 = bf16[512,256]{1,0:T(8,128)(2,1)} fusion(bf16[6144,256]{1,0:T(8,128)(2,1)} %convolution_convert_fusion, s32[1024]{0:T(1024)S(1)} %pad_clamp_fusion), kind=kCustom, calls=%fused_computation.2 | custom fusion | bytes 526336 | tf_op jit(solution)/shard_map/gather | solution.py:72
  92.1 0.0 copy-start.6
  92.2 6.6 %copy.33 = f32[12,512,256]{2,1,0:T(8,128)} copy(f32[12,512,256]{1,2,0:T(8,128)} %convolution_bitcast_fusion) | data formatting | bytes 12582912 | tf_op jit(solution)/shard_map/cji,cjf->cif/dot_general | solution.py:84
  98.8 0.0 copy-done.6
  98.8 1.8 fusion.20
  100.5 0.0 all-to-all-done.2
  100.5 6.0 %all-to-all-start.3 = ((bf16[32,16,256]{2,1,0:T(8,128)(2,1)}), bf16[32,16,256]{2,1,0:T(8,128)(2,1)}, u32[]{:S(2)}, u32[]{:S(2)}) async-start(bf16[32,16,256]{2,1,0:T(8,128)(2,1)} %fusion.20), calls=%async_computation.3 | async-start | bytes 524288 | tf_op jit(solution)/shard_map/all_to_all | solution.py:75
  106.5 6.6 %scatter_custom_fusion.1 = f32[6144,256]{1,0:T(8,128)} fusion(s32[512]{0:T(512)} %copy-done.8, f32[]{:T(128)} %constant.13.clone.1, bf16[512,256]{1,0:T(8,128)(2,1)S(1)} %bitcast.45, f32[512]{0:T(512)} %copy-done.7), kind=kCustom, calls=%fused_computation.23 | custom fusion | flops 393216 | bytes 6556160 | tf_op jit(solution)/shard_map/scatter-add | solution.py:79
  113.1 7.6 %fusion.1 = bf16[6144,256]{1,0:T(8,128)(2,1)} fusion(f32[6144,256]{1,0:T(8,128)} %bitcast.44, bf16[256,256]{1,0:T(8,128)(2,1)S(1)} %copy-done.4, f32[6144,256]{1,0:T(8,128)} %scatter_custom_fusion.1, f32[6144]{0:T(1024)} %fusion.28), kind=kOutput, calls=%fused_computation.11 | convolution fusion | flops 811597824 | bytes 15884288 | tf_op jit(solution)/shard_map/dot_general | solution.py:90
  120.7 0.0 copy-done.9
  120.7 40.5 %psum.15 = f32[256]{0:T(256)S(1)} all-reduce(f32[256]{0:T(256)S(1)} %copy-done.9), channel_id=1, replica_groups=mesh['group'=4,'inner'=8] {'group','inner'}, use_global_device_ids=true, to_apply=%region_4.5 | all-reduce | flops 256 | bytes 2048 | tf_op jit(solution)/shard_map/psum | solution.py:92
  161.2 0.6 broadcast_multiply_fusion.1
  161.7 44.1 %all-reduce.2.cloned.1.call-done = f32[256,256]{1,0:T(8,128)} async-done(((f32[256,256]{1,0:T(8,128)}), f32[256,256]{1,0:T(8,128)}) %all-reduce.2.cloned.1.call-update) | async-done | bytes 262160 | tf_op jit(solution)/shard_map/psum | solution.py:92
  205.8 1.7 broadcast_multiply_fusion
  207.5 0.0 all-to-all-done.3
  207.5 6.7 %scatter_custom_fusion.2 = f32[6144,256]{1,0:T(8,128)} fusion(s32[512]{0:T(512)} %reshape.207, f32[]{:T(128)} %constant.13.clone.1, bf16[512,256]{1,0:T(8,128)(2,1)} %bitcast.21), kind=kCustom, calls=%fused_computation.21 | custom fusion | flops 262144 | bytes 6554112 | tf_op jit(solution)/shard_map/scatter-add | solution.py:76
  214.2 4.8 %convert_element_type.67 = bf16[6144,256]{1,0:T(8,128)(2,1)} convert(f32[6144,256]{1,0:T(8,128)} %scatter_custom_fusion.2) | non-fusion elementwise | flops 1572864 | bytes 9437184 | tf_op jit(solution)/shard_map/convert_element_type | solution.py:78
  (6 shorter events, 0.0 us)
Async XLA Ops:
  7.2 24.6 %copy-start = (bf16[6144,256]{1,0:T(8,128)(2,1)S(1)}, bf16[6144,256]{1,0:T(8,128)(2,1)}, u32[]{:S(2)}) copy-start(bf16[6144,256]{1,0:T(8,128)(2,1)} %param.12) | copy-start | bytes 9437188
  8.7 14.4 %all-to-all-start = ((s32[32,1,16]{2,1,0:T(1,128)}), s32[32,1,16]{2,1,0:T(1,128)S(1)}, u32[]{:S(2)}, u32[]{:S(2)}) async-start(s32[32,1,16]{2,1,0:T(1,128)} %bitcast.4), calls=%async_computation | async-start | bytes 32768 | tf_op jit(solution)/shard_map/all_to_all | solution.py:42
  20.5 33.5 %copy-start.7 = (f32[512]{0:T(512)}, f32[512]{0:T(512)S(1)}, u32[]{:S(2)}) copy-start(f32[512]{0:T(512)S(1)} %broadcast_select_fusion) | copy-start | bytes 6148
  20.6 33.4 %copy-start.8 = (s32[512]{0:T(512)}, s32[512]{0:T(512)S(1)}, u32[]{:S(2)}) copy-start(s32[512]{0:T(512)S(1)} %reshape.191) | copy-start | bytes 6148
  23.1 4.6 %copy-start.5 = (s32[32,1,16]{2,1,0:T(1,128)}, s32[32,1,16]{2,1,0:T(1,128)S(1)}, u32[]{:S(2)}) copy-start(s32[32,1,16]{2,1,0:T(1,128)S(1)} %all-to-all-done) | copy-start | bytes 6148
  27.7 19.7 %all-to-all-start.1 = ((bf16[32,16,256]{2,1,0:T(8,128)(2,1)}), bf16[32,16,256]{2,1,0:T(8,128)(2,1)S(1)}, u32[]{:S(2)}, u32[]{:S(2)}) async-start(bf16[32,16,256]{2,1,0:T(8,128)(2,1)} %bitcast.48), calls=%async_computation.1 | async-start | bytes 524288 | tf_op jit(solution)/shard_map/all_to_all | solution.py:45
  39.0 24.0 %copy-start.4 = (bf16[256,256]{1,0:T(8,128)(2,1)S(1)}, bf16[256,256]{1,0:T(8,128)(2,1)}, u32[]{:S(2)}) copy-start(bf16[256,256]{1,0:T(8,128)(2,1)} %param.21) | copy-start | bytes 393220
  47.4 0.7 copy-start.3
  48.1 52.4 %all-to-all-start.2 = ((bf16[32,16,256]{2,1,0:T(8,128)(2,1)}), bf16[32,16,256]{2,1,0:T(8,128)(2,1)S(1)}, u32[]{:S(2)}, u32[]{:S(2)}) async-start(bf16[32,16,256]{2,1,0:T(8,128)(2,1)} %bitcast.46), calls=%async_computation.2 | async-start | bytes 524288 | tf_op jit(solution)/shard_map/all_to_all | solution.py:46
  54.0 151.8 %all-reduce.2.cloned.1.call-start = ((), (), s32[]{:S(2)}) async-start(), calls=%async_computation.4 | async-start | bytes 524288 | tf_op jit(solution)/shard_map/psum | solution.py:92
  63.0 10.1 %copy-start.1 = (f32[6144,256]{1,0:T(8,128)S(1)}, f32[6144,256]{1,0:T(8,128)}, u32[]{:S(2)}) copy-start(f32[6144,256]{1,0:T(8,128)} %scatter_custom_fusion) | copy-start | bytes 18874372
  71.4 1.7 copy-start.2
  92.1 6.6 %copy-start.6 = (f32[32,16]{1,0:T(8,128)S(1)}, f32[32,16]{1,0:T(8,128)}, u32[]{:S(2)}) copy-start(f32[32,16]{1,0:T(8,128)} %copy.34) | copy-start | bytes 6148
  100.5 106.9 %all-to-all-start.3 = ((bf16[32,16,256]{2,1,0:T(8,128)(2,1)}), bf16[32,16,256]{2,1,0:T(8,128)(2,1)}, u32[]{:S(2)}, u32[]{:S(2)}) async-start(bf16[32,16,256]{2,1,0:T(8,128)(2,1)} %fusion.20), calls=%async_computation.3 | async-start | bytes 524288 | tf_op jit(solution)/shard_map/all_to_all | solution.py:75
  113.1 7.6 %copy-start.9 = (f32[256]{0:T(256)S(1)}, f32[256]{0:T(256)}, u32[]{:S(2)}) copy-start(f32[256]{0:T(256)} %get-tuple-element.4) | copy-start | bytes 3076
Sparse Core Ops, SparseCore 0:
  79.5 126.2 all-reduce.1
where the time goes:
time: 227 us; the launch traced here: 226 us
  waiting for transfers between devices  45.8 us (20%)
  blocking collectives  40.5 us (18%)
  matrix products  37.8 us (17%)
  other arithmetic  35.1 us (15%)
  local copies, waits for them, and re-layouts  28.6 us (13%)
  starting transfers between devices  23.2 us (10%)
  between operations  14.8 us (7%)
    psum x1, waiting for transfers between devices, on_device(): lax.psum((weight_part, bias_part), ('group', 'inner'))  44.1 us
    psum x1, blocking collectives, on_device(): lax.psum((weight_part, bias_part), ('group', 'inner'))  40.5 us
    scatter-add x1, other arithmetic, on_device(): jax.ops.segment_sum(weights_col * got_emb.reshape(-1, width).astype(jnp.f...  8.96 us
    dot_general x1, matrix products, on_device(): jnp.dot(aggregate, layer_weight, preferred_element_type=jnp.float32)  8.45 us
    dot_general x1, matrix products, on_device(): jnp.einsum('cji,cjf->cif', adj_blocks, feat_grad.reshape(clusters, cluste...  8.25 us
    dot_general x1, matrix products, on_device(): jnp.dot(comp_grad, layer_weight.T, preferred_element_type=jnp.float32)  7.58 us
    all_to_all x1, starting transfers between devices, on_device(): lax.all_to_all(asked, ('group', 'inner'), split_axis=0, concat_axis=0, ti...  7.3 us
    dot_general x1, matrix products, on_device(): jnp.einsum('cij,cjf->cif', adj_blocks, node_feats.reshape(clusters, clust...  7.24 us
  transfers between devices with their start and end apart: 5, of which 2 were waited for; matrix products, arithmetic and copies ran while one was open for 36% of the time, Pallas kernels for 0%

commit v1 on v0

--- a/solution.py
+++ b/solution.py
@@ -1,8 +1,18 @@
+import functools
 import math
 import jax
 import jax.numpy as jnp
 from jax import lax
 from jax.sharding import PartitionSpec as P
+
+
+def pack_ends_in(local, bus_axis, dev_axis):
+    s_next = lax.psum(local, bus_axis)
+    y1 = lax.psum(s_next, axis_name=dev_axis)
+    return y1
+
+
+touch_run = functools.partial(pack_ends_in, bus_axis="inner", dev_axis="group")
 
 
 def gelu_slope(values):
@@ -89,7 +99,7 @@
     ).reshape(nodes_dev, width)
     back_sum = back_sum + jnp.dot(comp_grad, layer_weight.T, preferred_element_type=jnp.float32)
     input_grad = (back_sum * live_rows).astype(jnp.bfloat16)
-    weight_sum, bias_sum = lax.psum((weight_part, bias_part), ("group", "inner"))
+    weight_sum, bias_sum = touch_run((weight_part, bias_part))
     norm_factor = float(nodes_dev * groups * members) ** (-0.5)
     return (input_grad, weight_sum * norm_factor, bias_sum * norm_factor, owner_grad)
 

time: 227 us -> 202 us (0.89)
  blocking collectives: 40.5 us -> 23.5 us
  waiting for transfers between devices: 45.8 us -> 37.8 us
    psum x1 -> x2, blocking collectives: 40.5 us -> 23.5 us  [the longest x1 13.7 us: pack_ends_in(): s_next = lax.psum(local, bus_axis)]
    psum x1 -> x2, waiting for transfers between devices: 44.1 us -> 36 us  [the longest x1 22.6 us: pack_ends_in(): s_next = lax.psum(local, bus_axis)]
  transfers between devices with their start and end apart: 5 -> 6, of which waited for: 2 -> 3; matrix products, arithmetic and copies ran while one was open for 36% -> 41% of each run, Pallas kernels for 0% -> 0%
where the time goes in v1:
time: 202 us; the launch traced here: 201 us
  waiting for transfers between devices  37.8 us (19%)
  matrix products  37.8 us (19%)
  other arithmetic  35.1 us (17%)
  local copies, waits for them, and re-layouts  28.6 us (14%)
  blocking collectives  23.5 us (12%)
  starting transfers between devices  23.3 us (12%)
  between operations  14.8 us (7%)
    psum x1, waiting for transfers between devices, pack_ends_in(): s_next = lax.psum(local, bus_axis)  22.6 us
    psum x1, blocking collectives, pack_ends_in(): s_next = lax.psum(local, bus_axis)  13.7 us
    psum x1, waiting for transfers between devices, pack_ends_in(): y1 = lax.psum(s_next, axis_name=dev_axis)  13.5 us
    psum x1, blocking collectives, pack_ends_in(): y1 = lax.psum(s_next, axis_name=dev_axis)  9.82 us
    scatter-add x1, other arithmetic, on_device(): jax.ops.segment_sum(weights_col * got_emb.reshape(-1, width).astype(jnp.f...  8.97 us
    dot_general x1, matrix products, on_device(): jnp.dot(aggregate, layer_weight, preferred_element_type=jnp.float32)  8.45 us
    dot_general x1, matrix products, on_device(): jnp.einsum('cji,cjf->cif', adj_blocks, feat_grad.reshape(clusters, cluste...  8.24 us
    dot_general x1, matrix products, on_device(): jnp.dot(comp_grad, layer_weight.T, preferred_element_type=jnp.float32)  7.56 us
  transfers between devices with their start and end apart: 6, of which 3 were waited for; matrix products, arithmetic and copies ran while one was open for 41% of the time, Pallas kernels for 0%

profile of v1, /device:TPU:0, one launch (start us, length us, event | category | flops | bytes accessed | tf_op | source)
XLA Modules:
  0.0 200.9 jit_solution(7016713375051704175)
XLA Ops:
  7.2 0.0 copy-start
  7.2 1.5 copy.31
  8.7 7.3 %all-to-all-start = ((s32[32,1,16]{2,1,0:T(1,128)}), s32[32,1,16]{2,1,0:T(1,128)S(1)}, u32[]{:S(2)}, u32[]{:S(2)}) async-start(s32[32,1,16]{2,1,0:T(1,128)} %bitcast.4), calls=%async_computation | async-start | bytes 32768 | tf_op jit(solution)/shard_map/all_to_all | solution.py:52
  16.0 0.7 iota_compare_fusion
  16.7 0.7 bitcast_select_fusion
  17.4 0.8 copy.30
  18.8 0.1 copy.29
  18.9 0.1 lt.61
  19.0 0.8 copy.28
  19.8 0.1 reshape.183
  19.9 0.1 squeeze.12
  19.9 0.6 fusion.28
  20.5 0.0 copy-start.7
  20.6 0.1 reshape.191
  20.6 0.0 copy-start.8
  20.6 0.7 copy.34
  21.3 1.8 all-to-all-done
  23.1 0.0 copy-start.5
  23.1 0.1 reshape.167
  23.2 4.5 %gather_fusion = bf16[512,256]{1,0:T(8,128)(2,1)} fusion(bf16[6144,256]{1,0:T(8,128)(2,1)} %param.19, s32[1024]{0:T(1024)S(1)} %pad_clamp_fusion.1), kind=kCustom, calls=%fused_computation | custom fusion | bytes 526336 | tf_op jit(solution)/shard_map/gather | solution.py:53
  27.7 0.0 copy-done.5
  27.7 4.1 %all-to-all-start.1 = ((bf16[32,16,256]{2,1,0:T(8,128)(2,1)}), bf16[32,16,256]{2,1,0:T(8,128)(2,1)S(1)}, u32[]{:S(2)}, u32[]{:S(2)}) async-start(bf16[32,16,256]{2,1,0:T(8,128)(2,1)} %bitcast.48), calls=%async_computation.1 | async-start | bytes 524288 | tf_op jit(solution)/shard_map/all_to_all | solution.py:55
  31.8 0.0 copy-done
  31.8 7.2 %fusion.30 = f32[12,512,256]{2,1,0:T(8,128)} fusion(bf16[12,512,512]{2,1,0:T(8,128)(2,1)} %bitcast.40, bf16[12,512,256]{2,1,0:T(8,128)(2,1)S(1)} %bitcast.39), kind=kOutput, calls=%fused_computation.58 | convolution fusion | flops 1610612736 | bytes 15728640 | tf_op jit(solution)/shard_map/cij,cjf->cif/dot_general | solution.py:61
  39.0 0.5 broadcast.135
  39.5 2.0 %reduce.3 = s32[32,16]{1,0:T(8,128)} reduce(s32[32,1,16]{2,1,0:T(1,128)} %copy-done.5, s32[]{:T(128)} %broadcast.135), dimensions={1}, to_apply=%all_to_all.18.reduce_sub_computation.3 | reduce | bytes 4100 | tf_op jit(solution)/shard_map/all_to_all | solution.py:52
  41.5 1.4 reshape.207
  42.9 4.5 %gather_fusion.1 = bf16[512,256]{1,0:T(8,128)(2,1)} fusion(bf16[6144,256]{1,0:T(8,128)(2,1)} %param.20, s32[1024]{0:T(1024)S(1)} %pad_clamp_fusion.1), kind=kCustom, calls=%fused_computation.1 | custom fusion | bytes 526336 | tf_op jit(solution)/shard_map/gather | solution.py:54
  47.4 0.0 all-to-all-done.1
  47.4 0.7 copy-done.3
  48.1 5.8 %all-to-all-start.2 = ((bf16[32,16,256]{2,1,0:T(8,128)(2,1)}), bf16[32,16,256]{2,1,0:T(8,128)(2,1)S(1)}, u32[]{:S(2)}, u32[]{:S(2)}) async-start(bf16[32,16,256]{2,1,0:T(8,128)(2,1)} %bitcast.46), calls=%async_computation.2 | async-start | bytes 524288 | tf_op jit(solution)/shard_map/all_to_all | solution.py:56
  53.9 0.0 all-reduce.3.cloned.1.call-start
  54.0 0.0 copy-done.7
  54.0 0.0 copy-done.8
  54.0 9.0 %scatter_custom_fusion = f32[6144,256]{1,0:T(8,128)} fusion(f32[6144,256]{1,0:T(8,128)} %bitcast.42, s32[512]{0:T(512)S(1)} %reshape.191, bf16[512,256]{1,0:T(8,128)(2,1)} %bitcast.47, f32[512]{0:T(512)S(1)} %broadcast_select_fusion), kind=kCustom, calls=%fused_computation.36 | custom fusion | flops 393216 | bytes 6555648 | tf_op jit(solution)/shard_map/scatter-add | solution.py:67
  63.0 0.0 copy-done.4
  63.0 8.5 %fusion.29 = (f32[256]{0:T(256)}, bf16[6144,256]{1,0:T(8,128)(2,1)S(1)}) fusion(f32[6144]{0:T(1024)} %fusion.28, f32[256]{0:T(256)} %param.22, bf16[256,256]{1,0:T(8,128)(2,1)S(1)} %copy-done.4, f32[6144,256]{1,0:T(8,128)} %scatter_custom_fusion, bf16[6144,256]{1,0:T(8,128)(2,1)} %param.23), kind=kOutput, calls=%fused_computation.57 | convolution fusion | flops 843054848 | bytes 12740608 | tf_op jit(solution)/shard_map/dot_general | solution.py:73
  71.4 1.7 copy-done.2
  73.1 0.0 copy-done.1
  73.1 1.7 fusion.14
  74.8 4.6 %convolution_convert_fusion = bf16[6144,256]{1,0:T(8,128)(2,1)} fusion(bf16[256,256]{1,0:T(8,128)(2,1)S(1)} %copy-done.4, bf16[6144,256]{1,0:T(8,128)(2,1)} %copy-done.2), kind=kOutput, calls=%fused_computation.12 | convolution fusion | flops 806879232 | bytes 6422528 | tf_op jit(solution)/shard_map/dot_general | solution.py:79
  79.4 0.0 all-reduce.3.cloned.1.call-update
  79.4 8.2 %convolution_bitcast_fusion = f32[12,512,256]{1,2,0:T(8,128)} fusion(bf16[12,512,256]{2,1,0:T(8,128)(2,1)} %bitcast.43, bf16[12,512,512]{2,1,0:T(8,128)(2,1)} %bitcast.41), kind=kOutput, calls=%fused_computation.25 | convolution fusion | flops 1610612736 | bytes 15728640 | tf_op jit(solution)/shard_map/cji,cjf->cif/dot_general | solution.py:94
  87.7 4.5 %gather_fusion.2 = bf16[512,256]{1,0:T(8,128)(2,1)} fusion(bf16[6144,256]{1,0:T(8,128)(2,1)} %convolution_convert_fusion, s32[1024]{0:T(1024)S(1)} %pad_clamp_fusion), kind=kCustom, calls=%fused_computation.2 | custom fusion | bytes 526336 | tf_op jit(solution)/shard_map/gather | solution.py:82
  92.1 6.6 %copy.33 = f32[12,512,256]{2,1,0:T(8,128)} copy(f32[12,512,256]{1,2,0:T(8,128)} %convolution_bitcast_fusion) | data formatting | bytes 12582912 | tf_op jit(solution)/shard_map/cji,cjf->cif/dot_general | solution.py:94
  98.8 0.0 copy-done.6
  98.8 1.8 fusion.20
  100.6 0.0 all-to-all-done.2
  100.6 6.0 %all-to-all-start.3 = ((bf16[32,16,256]{2,1,0:T(8,128)(2,1)}), bf16[32,16,256]{2,1,0:T(8,128)(2,1)}, u32[]{:S(2)}, u32[]{:S(2)}) async-start(bf16[32,16,256]{2,1,0:T(8,128)(2,1)} %fusion.20), calls=%async_computation.3 | async-start | bytes 524288 | tf_op jit(solution)/shard_map/all_to_all | solution.py:85
  106.6 0.0 all-reduce.5.cloned.1.call-start
  106.6 6.6 %scatter_custom_fusion.1 = f32[6144,256]{1,0:T(8,128)} fusion(s32[512]{0:T(512)} %copy-done.8, f32[]{:T(128)} %constant.13.clone.1, bf16[512,256]{1,0:T(8,128)(2,1)S(1)} %bitcast.45, f32[512]{0:T(512)} %copy-done.7), kind=kCustom, calls=%fused_computation.23 | custom fusion | flops 393216 | bytes 6556160 | tf_op jit(solution)/shard_map/scatter-add | solution.py:89
  113.2 22.6 %all-reduce.3.cloned.1.call-done = f32[256,256]{1,0:T(8,128)} async-done(((f32[256,256]{1,0:T(8,128)}), f32[256,256]{1,0:T(8,128)}) %all-reduce.3.cloned.1.call-update) | async-done | bytes 262160 | tf_op jit(solution)/shard_map/psum | solution.py:10
  135.7 0.0 all-reduce.5.cloned.1.call-update
  135.8 0.0 copy-start.9
  135.8 7.6 %fusion.1 = bf16[6144,256]{1,0:T(8,128)(2,1)} fusion(f32[6144,256]{1,0:T(8,128)} %bitcast.44, bf16[256,256]{1,0:T(8,128)(2,1)S(1)} %copy-done.4, f32[6144,256]{1,0:T(8,128)} %scatter_custom_fusion.1, f32[6144]{0:T(1024)} %fusion.28), kind=kOutput, calls=%fused_computation.11 | convolution fusion | flops 811597824 | bytes 15884288 | tf_op jit(solution)/shard_map/dot_general | solution.py:100
  143.3 0.0 copy-done.9
  143.3 13.7 %psum.30 = f32[256]{0:T(256)S(1)} all-reduce(f32[256]{0:T(256)S(1)} %copy-done.9), channel_id=1, replica_groups=mesh['group'=4,'inner'=8] {'inner'}, use_global_device_ids=true, to_apply=%region_5.6 | all-reduce | flops 256 | bytes 2048 | tf_op jit(solution)/shard_map/psum | solution.py:10
  157.0 9.8 %psum.31 = f32[256]{0:T(256)S(1)} all-reduce(f32[256]{0:T(256)S(1)} %psum.30), channel_id=1, replica_groups=mesh['group'=4,'inner'=8] {'group'}, use_global_device_ids=true, to_apply=%region_6.7 | all-reduce | flops 256 | bytes 2048 | tf_op jit(solution)/shard_map/psum | solution.py:11
  166.8 0.6 broadcast_multiply_fusion.1
  167.4 13.5 %all-reduce.5.cloned.1.call-done = f32[256,256]{1,0:T(8,128)} async-done(((f32[256,256]{1,0:T(8,128)}), f32[256,256]{1,0:T(8,128)}) %all-reduce.5.cloned.1.call-update) | async-done | bytes 262160 | tf_op jit(solution)/shard_map/psum | solution.py:11
  180.8 1.7 broadcast_multiply_fusion
  182.5 0.0 all-to-all-done.3
  182.5 6.8 %scatter_custom_fusion.2 = f32[6144,256]{1,0:T(8,128)} fusion(s32[512]{0:T(512)} %reshape.207, f32[]{:T(128)} %constant.13.clone.1, bf16[512,256]{1,0:T(8,128)(2,1)} %bitcast.21), kind=kCustom, calls=%fused_computation.21 | custom fusion | flops 262144 | bytes 6554112 | tf_op jit(solution)/shard_map/scatter-add | solution.py:86
  189.3 4.8 %convert_element_type.67 = bf16[6144,256]{1,0:T(8,128)(2,1)} convert(f32[6144,256]{1,0:T(8,128)} %scatter_custom_fusion.2) | non-fusion elementwise | flops 1572864 | bytes 9437184 | tf_op jit(solution)/shard_map/convert_element_type | solution.py:88
  (10 shorter events, 0.0 us)
Async XLA Ops:
  7.2 24.6 %copy-start = (bf16[6144,256]{1,0:T(8,128)(2,1)S(1)}, bf16[6144,256]{1,0:T(8,128)(2,1)}, u32[]{:S(2)}) copy-start(bf16[6144,256]{1,0:T(8,128)(2,1)} %param.12) | copy-start | bytes 9437188
  8.7 14.4 %all-to-all-start = ((s32[32,1,16]{2,1,0:T(1,128)}), s32[32,1,16]{2,1,0:T(1,128)S(1)}, u32[]{:S(2)}, u32[]{:S(2)}) async-start(s32[32,1,16]{2,1,0:T(1,128)} %bitcast.4), calls=%async_computation | async-start | bytes 32768 | tf_op jit(solution)/shard_map/all_to_all | solution.py:52
  20.5 33.4 %copy-start.7 = (f32[512]{0:T(512)}, f32[512]{0:T(512)S(1)}, u32[]{:S(2)}) copy-start(f32[512]{0:T(512)S(1)} %broadcast_select_fusion) | copy-start | bytes 6148
  20.6 33.4 %copy-start.8 = (s32[512]{0:T(512)}, s32[512]{0:T(512)S(1)}, u32[]{:S(2)}) copy-start(s32[512]{0:T(512)S(1)} %reshape.191) | copy-start | bytes 6148
  23.1 4.6 %copy-start.5 = (s32[32,1,16]{2,1,0:T(1,128)}, s32[32,1,16]{2,1,0:T(1,128)S(1)}, u32[]{:S(2)}) copy-start(s32[32,1,16]{2,1,0:T(1,128)S(1)} %all-to-all-done) | copy-start | bytes 6148
  27.7 19.7 %all-to-all-start.1 = ((bf16[32,16,256]{2,1,0:T(8,128)(2,1)}), bf16[32,16,256]{2,1,0:T(8,128)(2,1)S(1)}, u32[]{:S(2)}, u32[]{:S(2)}) async-start(bf16[32,16,256]{2,1,0:T(8,128)(2,1)} %bitcast.48), calls=%async_computation.1 | async-start | bytes 524288 | tf_op jit(solution)/shard_map/all_to_all | solution.py:55
  39.0 24.0 %copy-start.4 = (bf16[256,256]{1,0:T(8,128)(2,1)S(1)}, bf16[256,256]{1,0:T(8,128)(2,1)}, u32[]{:S(2)}) copy-start(bf16[256,256]{1,0:T(8,128)(2,1)} %param.21) | copy-start | bytes 393220
  47.4 0.7 copy-start.3
  48.1 52.5 %all-to-all-start.2 = ((bf16[32,16,256]{2,1,0:T(8,128)(2,1)}), bf16[32,16,256]{2,1,0:T(8,128)(2,1)S(1)}, u32[]{:S(2)}, u32[]{:S(2)}) async-start(bf16[32,16,256]{2,1,0:T(8,128)(2,1)} %bitcast.46), calls=%async_computation.2 | async-start | bytes 524288 | tf_op jit(solution)/shard_map/all_to_all | solution.py:56
  53.9 81.8 %all-reduce.3.cloned.1.call-start = ((), (), s32[]{:S(2)}) async-start(), calls=%async_computation.4 | async-start | bytes 524288 | tf_op jit(solution)/shard_map/psum | solution.py:10
  63.0 10.1 %copy-start.1 = (f32[6144,256]{1,0:T(8,128)S(1)}, f32[6144,256]{1,0:T(8,128)}, u32[]{:S(2)}) copy-start(f32[6144,256]{1,0:T(8,128)} %scatter_custom_fusion) | copy-start | bytes 18874372
  71.4 1.7 copy-start.2
  92.1 6.6 %copy-start.6 = (f32[32,16]{1,0:T(8,128)S(1)}, f32[32,16]{1,0:T(8,128)}, u32[]{:S(2)}) copy-start(f32[32,16]{1,0:T(8,128)} %copy.34) | copy-start | bytes 6148
  100.6 82.0 %all-to-all-start.3 = ((bf16[32,16,256]{2,1,0:T(8,128)(2,1)}), bf16[32,16,256]{2,1,0:T(8,128)(2,1)}, u32[]{:S(2)}, u32[]{:S(2)}) async-start(bf16[32,16,256]{2,1,0:T(8,128)(2,1)} %fusion.20), calls=%async_computation.3 | async-start | bytes 524288 | tf_op jit(solution)/shard_map/all_to_all | solution.py:85
  106.6 74.3 %all-reduce.5.cloned.1.call-start = ((), (), s32[]{:S(2)}) async-start(), calls=%async_computation.5 | async-start | bytes 524288 | tf_op jit(solution)/shard_map/psum | solution.py:11
  135.8 7.6 %copy-start.9 = (f32[256]{0:T(256)S(1)}, f32[256]{0:T(256)}, u32[]{:S(2)}) copy-start(f32[256]{0:T(256)} %get-tuple-element.4) | copy-start | bytes 3076
Sparse Core Ops, SparseCore 0:
  79.5 56.1 all-reduce.2
  138.9 41.8 all-reduce.4
